TPU v7x, 128 devices: a whole 4x4x4 slice. The times are simulated.
128 devices in a mesh: row: 8 (over z, core), col: 16 (over x, y).
Axes of the slice: x: 4, y: 4, z: 4, core: 2. Of those that a mesh axis runs over, the one named last changes fastest.
Arguments:
- front_panel: float32 [40960, 512], P('row', 'col'), may hold values from -16 to 48, as said below
- front_slab: float32 [40960, 8192], P('row', 'col'), may hold values from -6 to 6
- child_one: bfloat16 [8192, 8192], P('col', 'row'), may hold values from -6 to 6
- child_two: bfloat16 [8192, 8192], P('col', 'row'), may hold values from -6 to 6
- map_one: int32 [32], replicated, may hold values from 0 to 159, as said below
- map_two: int32 [32], replicated, may hold values from 0 to 159, as said below
Outputs:
- factor_panel: float32 [40960, 512], P('row', 'col')
- slab_out: float32 [40960, 8192], P('row', 'col')
Inputs may be any that keep to these rules, and one draw needn't show every extreme that they name: `front_panel`: its first 512 rows are, in all 512 columns, a symmetric positive definite block. `map_one`: distinct root row blocks. Of the 20 blocks of one index of row (numbers k * 20 to (k + 1) * 20 - 1) at most 8 are named, and exactly 8 for some index of row. `map_two`: as map_one, drawn independently.
All inputs are finite; a program needn't handle non-finite values.
Results may differ from a plain program's by a relative error of at most 0.0003.
Values may be sent and summed in bfloat16 or wider, within the bound.
A program may use at most 192 MiB of HBM per device.

v0:
```python
import jax
import jax.numpy as jnp
from jax import lax
from jax.sharding import PartitionSpec as P

P_SIZE = 256
BLK = 256


def from_root(value, axis, source):
    kept = jnp.where(lax.axis_index(axis) == source, value, 0).astype(value.dtype)
    return lax.psum(kept, axis)


def inverse_factor(block):
    lower = jnp.linalg.cholesky(block)
    identity = jnp.eye(P_SIZE, dtype=jnp.float32)
    return jax.scipy.linalg.solve_triangular(lower, identity, lower=True)


def diagonal_work(top):
    highest = lax.Precision.HIGHEST
    inverse_one = inverse_factor(top[:P_SIZE, :P_SIZE])
    first_top = jnp.dot(
        top[P_SIZE:, :P_SIZE], inverse_one.T, precision=highest, preferred_element_type=jnp.float32
    )
    second_top = top[P_SIZE:, P_SIZE:] - jnp.dot(
        first_top, first_top.T, precision=highest, preferred_element_type=jnp.float32
    )
    inverse_two = inverse_factor(second_top)
    return (inverse_one, first_top, inverse_two)


def panel_rows(panel, inverse_one, first_top, inverse_two):
    highest = lax.Precision.HIGHEST
    first_cols = jnp.dot(
        panel[:, :P_SIZE], inverse_one.T, precision=highest, preferred_element_type=jnp.float32
    )
    second_in = panel[:, P_SIZE:] - jnp.dot(
        first_cols, first_top.T, precision=highest, preferred_element_type=jnp.float32
    )
    second_cols = jnp.dot(
        second_in, inverse_two.T, precision=highest, preferred_element_type=jnp.float32
    )
    return jnp.concatenate([first_cols, second_cols], 1)


def routing(mapping, local_blocks, row_count):
    owner = mapping // local_blocks
    owner_hot = (owner[:, None] == jnp.arange(row_count, dtype=jnp.int32)[None, :]).astype(
        jnp.int32
    )
    rank = jnp.sum(owner_hot * (jnp.cumsum(owner_hot, 0) - 1), 1)
    return (owner, rank, mapping % local_blocks)


def per_device(front_panel, front_slab, child_one, child_two, map_one, map_two):
    rows_dev = front_slab.shape[0]
    slab_width = front_slab.shape[1]
    panel_width = front_panel.shape[1]
    child_blocks = map_one.shape[0]
    child_local = child_one.shape[0]
    row_count = lax.axis_size("row")
    col_count = lax.axis_size("col")
    row_rank = lax.axis_index("row")
    col_rank = lax.axis_index("col")
    piece = slab_width // row_count
    local_blocks = rows_dev // BLK
    capacity = 2 * child_blocks // row_count

    def split_columns(child):
        return child.reshape(child_local, col_count, piece)

    got_one, got_two = (
        lax.all_to_all(split_columns(child_one), "col", split_axis=1, concat_axis=0, tiled=True),
        lax.all_to_all(split_columns(child_two), "col", split_axis=1, concat_axis=0, tiled=True),
    )

    def send_rows(received, mapping):
        owner, rank, target = routing(mapping, local_blocks, row_count)
        slot = owner * capacity + rank
        select = (
            slot[None, :] == jnp.arange(row_count * capacity, dtype=jnp.int32)[:, None]
        ).astype(jnp.bfloat16)
        blocks = received.reshape(child_blocks, BLK * piece)
        packed = jnp.dot(select, blocks, preferred_element_type=jnp.float32).astype(jnp.bfloat16)
        return packed.reshape(row_count * capacity * BLK, piece)

    arrived_one, arrived_two = (
        lax.all_to_all(send_rows(got_one, map_one), "row", split_axis=0, concat_axis=1, tiled=True),
        lax.all_to_all(send_rows(got_two, map_two), "row", split_axis=0, concat_axis=1, tiled=True),
    )

    def place(arrived, mapping):
        owner, rank, target = routing(mapping, local_blocks, row_count)
        mine = (owner == row_rank)[None, :, None]
        at_block = target[None, :, None] == jnp.arange(local_blocks, dtype=jnp.int32)[:, None, None]
        at_slot = rank[None, :, None] == jnp.arange(capacity, dtype=jnp.int32)[None, None, :]
        placing = jnp.sum((at_block & at_slot & mine).astype(jnp.int32), 1).astype(jnp.bfloat16)
        added = jnp.dot(
            placing, arrived.reshape(capacity, BLK * slab_width), preferred_element_type=jnp.float32
        )
        return added.reshape(rows_dev, slab_width)

    assembled = front_slab + place(arrived_one, map_one) + place(arrived_two, map_two)
    gathered = lax.all_gather(front_panel, "col", axis=1, tiled=True)
    top = gathered[: 2 * P_SIZE]
    top = from_root(top, "row", 0)
    inverse_one, first_top, inverse_two = diagonal_work(top)
    factor = panel_rows(gathered, inverse_one, first_top, inverse_two)
    factor_out = lax.dynamic_slice_in_dim(factor, col_rank * panel_width, panel_width, 1)
    global_rows = row_rank * rows_dev + jnp.arange(rows_dev, dtype=jnp.int32)
    masked = factor * (global_rows >= 2 * P_SIZE)[:, None].astype(jnp.float32)
    wanted = (
        2 * P_SIZE
        + col_rank * slab_width
        + jnp.arange(slab_width, dtype=jnp.int32)
        - row_rank * rows_dev
    )
    valid = ((wanted >= 0) & (wanted < rows_dev))[:, None].astype(jnp.float32)
    picked = jnp.take(factor, jnp.clip(wanted, 0, rows_dev - 1), axis=0) * valid
    slab_rows = lax.psum(picked, "row")
    update = jnp.dot(
        masked, slab_rows.T, precision=lax.Precision.HIGHEST, preferred_element_type=jnp.float32
    )
    return (factor_out, assembled - update)


def solution(mesh):
    in_specs = (P("row", "col"), P("row", "col"), P("col", "row"), P("col", "row"), P(), P())
    out_specs = (P("row", "col"), P("row", "col"))
    return jax.shard_map(
        per_device, mesh=mesh, in_specs=in_specs, out_specs=out_specs, check_vma=False
    )
```

profile of v0, /device:TPU:0, one launch (start us, length us, event | category | flops | bytes accessed | tf_op | source)
XLA Modules:
  0.0 495.1 jit_solution(5786572889173300262)
XLA Ops:
  7.9 2.3 copy.39
  10.2 7.1 %all-to-all-start = ((bf16[512,16,64]{0,2,1:T(8,128)(2,1)}), bf16[512,16,64]{0,2,1:T(8,128)(2,1)S(1)}, u32[]{:S(2)}, u32[]{:S(2)}) async-start(bf16[512,16,64]{0,2,1:T(8,128)(2,1)} %bitcast.11), calls=%async_computation | async-start | bytes 2097152 | tf_op jit(solution)/shard_map/all_to_all | solution.py:75
  18.7 19.1 %all-to-all-done = bf16[512,16,64]{0,2,1:T(8,128)(2,1)S(1)} async-done(((bf16[512,16,64]{0,2,1:T(8,128)(2,1)}), bf16[512,16,64]{0,2,1:T(8,128)(2,1)S(1)}, u32[]{:S(2)}, u32[]{:S(2)}) %all-to-all-start) | async-done | bytes 1048608 | tf_op jit(solution)/shard_map/all_to_all | solution.py:75
  37.8 6.6 %all-to-all-start.2 = ((bf16[512,16,64]{0,2,1:T(8,128)(2,1)}), bf16[512,16,64]{0,2,1:T(8,128)(2,1)S(1)}, u32[]{:S(2)}, u32[]{:S(2)}) async-start(bf16[512,16,64]{0,2,1:T(8,128)(2,1)} %bitcast.15), calls=%async_computation.2 | async-start | bytes 2097152 | tf_op jit(solution)/shard_map/all_to_all | solution.py:76
  44.8 2.0 copy.40
  46.8 2.5 reshape.193
  49.3 1.9 convolution_convert_fusion.1
  51.2 5.5 %all_to_all.49 = bf16[8,2048,64]{2,1,0:T(8,128)(2,1)} reshape(bf16[64,16384]{1,0:T(8,128)(2,1)S(1)} %convolution_convert_fusion.1) | data formatting | bytes 4194304 | tf_op jit(solution)/shard_map/all_to_all | solution.py:90
  56.7 4.8 copy.41
  61.5 6.5 %all-to-all-start.1 = ((bf16[8,2048,64]{1,2,0:T(8,128)(2,1)}), bf16[8,2048,64]{1,2,0:T(8,128)(2,1)S(1)}, u32[]{:S(2)}, u32[]{:S(2)}) async-start(bf16[8,2048,64]{1,2,0:T(8,128)(2,1)} %copy.41), calls=%async_computation.1 | async-start | bytes 4194304 | tf_op jit(solution)/shard_map/all_to_all | solution.py:90
  68.4 1.8 copy.44
  70.2 2.8 reshape.197
  73.1 2.0 convolution_convert_fusion
  75.1 6.5 %all_to_all.55 = bf16[8,2048,64]{2,1,0:T(8,128)(2,1)} reshape(bf16[64,16384]{1,0:T(8,128)(2,1)} %convolution_convert_fusion) | data formatting | bytes 4194304 | tf_op jit(solution)/shard_map/all_to_all | solution.py:91
  81.6 4.8 copy.45
  86.4 8.9 %all-to-all-done.1 = bf16[8,2048,64]{1,2,0:T(8,128)(2,1)S(1)} async-done(((bf16[8,2048,64]{1,2,0:T(8,128)(2,1)}), bf16[8,2048,64]{1,2,0:T(8,128)(2,1)S(1)}, u32[]{:S(2)}, u32[]{:S(2)}) %all-to-all-start.1) | async-done | bytes 2097184 | tf_op jit(solution)/shard_map/all_to_all | solution.py:90
  95.2 4.3 all-to-all-start.3
  100.8 4.2 copy.42
  105.0 5.0 %reshape.232 = bf16[1048576]{0:T(1024)(128)(2,1)S(1)} reshape(bf16[2048,8,64]{2,1,0:T(8,128)(2,1)} %copy.42) | data formatting | bytes 4194304
  110.1 2.2 reshape.194
  112.3 7.9 %fusion.38 = f32[20,131072]{1,0:T(8,128)} fusion(bf16[8,131072]{1,0:T(8,128)(2,1)} %reshape.194, s32[20,8]{1,0:T(8,128)S(1)} %convert_reduce_fusion.1), kind=kOutput, calls=%fused_computation.86 | convolution fusion | flops 41943200 | bytes 12583552 | tf_op jit(solution)/shard_map/dot_general | solution.py:100
  120.2 10.5 %reshape.195 = f32[5120,512]{1,0:T(8,128)} reshape(f32[20,131072]{1,0:T(8,128)} %fusion.38) | data formatting | bytes 20971520 | tf_op jit(solution)/shard_map/reshape | solution.py:103
  130.7 5.6 %copy.46 = bf16[2048,8,64]{2,1,0:T(8,128)(2,1)} copy(bf16[2048,8,64]{0,2,1:T(8,128)(2,1)} %bitcast.18) | data formatting | bytes 4194304 | tf_op jit(solution)/shard_map/all_to_all | solution.py:91
  136.4 5.0 %reshape.230 = bf16[1048576]{0:T(1024)(128)(2,1)S(1)} reshape(bf16[2048,8,64]{2,1,0:T(8,128)(2,1)} %copy.46) | data formatting | bytes 4194304
  141.4 2.2 reshape.198
  143.6 2.3 slice_select_fusion
  146.0 7.9 %fusion.36 = f32[20,131072]{1,0:T(8,128)} fusion(bf16[8,131072]{1,0:T(8,128)(2,1)} %reshape.198, s32[20,8]{1,0:T(8,128)S(1)} %convert_reduce_fusion), kind=kOutput, calls=%fused_computation.84 | convolution fusion | flops 41943200 | bytes 12583552 | tf_op jit(solution)/shard_map/dot_general | solution.py:100
  153.9 11.0 %reshape.199 = f32[5120,512]{1,0:T(8,128)} reshape(f32[20,131072]{1,0:T(8,128)} %fusion.36) | data formatting | bytes 20971520 | tf_op jit(solution)/shard_map/reshape | solution.py:103
  164.9 45.9 %all-reduce.4.cloned.1.call-done = f32[512,512]{0,1:T(8,128)} async-done(((f32[512,512]{0,1:T(8,128)}), f32[512,512]{0,1:T(8,128)}) %all-reduce.4.cloned.1.call-update) | async-done | bytes 1048592 | tf_op jit(solution)/shard_map/psum | solution.py:12
  213.1 11.7 %cholesky.130 = f32[128,128]{1,0:T(8,128)S(1)} custom-call(f32[128,128]{1,0:T(8,128)S(1)} %cholesky.194), custom_call_target="Cholesky" | custom-call | tf_op jit(solution)/shard_map/jit(cholesky)/cholesky | solution.py:16
  224.8 9.8 %custom-call.13 = f32[1,128,128]{1,2,0:T(8,128)S(1)} custom-call(f32[1,128,128]{2,1,0:T(8,128)S(1)} %get-tuple-element.51), custom_call_target="InvertDiagBlocksLowerTriangular" | custom-call | tf_op jit(solution)/shard_map/jit(cholesky)/cholesky | solution.py:16
  235.1 11.7 %cholesky.147 = f32[128,128]{1,0:T(8,128)S(1)} custom-call(f32[128,128]{1,0:T(8,128)S(1)} %convolution_subtract_fusion.5), custom_call_target="Cholesky" | custom-call | tf_op jit(solution)/shard_map/jit(cholesky)/cholesky | solution.py:16
  248.9 3.9 while.4
  252.8 19.8 %custom-call.14 = f32[2,128,128]{1,2,0:T(8,128)S(1)} custom-call(f32[2,128,128]{2,1,0:T(8,128)S(1)} %get-tuple-element.18), custom_call_target="InvertDiagBlocksLowerTriangular" | custom-call | tf_op jit(solution)/shard_map/jit(_solve_triangular)/triangular_solve | solution.py:18
  274.8 11.7 %cholesky.164 = f32[128,128]{1,0:T(8,128)S(1)} custom-call(f32[128,128]{1,0:T(8,128)S(1)} %cholesky.197), custom_call_target="Cholesky" | custom-call | tf_op jit(solution)/shard_map/jit(cholesky)/cholesky | solution.py:16
  286.5 9.8 %custom-call.15 = f32[1,128,128]{1,2,0:T(8,128)S(1)} custom-call(f32[1,128,128]{2,1,0:T(8,128)S(1)} %get-tuple-element.47), custom_call_target="InvertDiagBlocksLowerTriangular" | custom-call | tf_op jit(solution)/shard_map/jit(cholesky)/cholesky | solution.py:16
  296.8 11.7 %cholesky.181 = f32[128,128]{1,0:T(8,128)S(1)} custom-call(f32[128,128]{1,0:T(8,128)S(1)} %convolution_subtract_fusion.4), custom_call_target="Cholesky" | custom-call | tf_op jit(solution)/shard_map/jit(cholesky)/cholesky | solution.py:16
  311.3 4.1 while.5
  315.4 19.9 %custom-call.16 = f32[2,128,128]{1,2,0:T(8,128)S(1)} custom-call(f32[2,128,128]{2,1,0:T(8,128)S(1)} %get-tuple-element.19), custom_call_target="InvertDiagBlocksLowerTriangular" | custom-call | tf_op jit(solution)/shard_map/jit(_solve_triangular)/triangular_solve | solution.py:18
  336.2 6.7 %fusion.4 = f32[256,5120]{1,0:T(8,128)S(1)} fusion(f32[5120,512]{0,1:T(8,128)} %all-gather.2.cloned.1.call-done, f32[128,256]{1,0:T(8,128)S(1)} %fusion.26, f32[128,256]{1,0:T(8,128)S(1)} %fusion.19), kind=kOutput, calls=%fused_computation.14 | convolution fusion | flops 4026597376 | bytes 10747904 | tf_op jit(solution)/shard_map/dot_general | solution.py:36
  342.9 9.0 %convolution_subtract_fusion = f32[5120,256]{0,1:T(8,128)S(1)} fusion(f32[256,5120]{1,0:T(8,128)S(1)} %fusion.4, f32[256,256]{1,0:T(8,128)S(1)} %fusion.8, f32[5120,512]{0,1:T(8,128)} %all-gather.2.cloned.1.call-done), kind=kOutput, calls=%fused_computation.13 | convolution fusion | flops 4027842560 | bytes 15990784 | tf_op jit(solution)/shard_map/dot_general | solution.py:39
  351.9 6.5 %fusion.10 = f32[5120,256]{0,1:T(8,128)} fusion(f32[5120,256]{0,1:T(8,128)S(1)} %convolution_subtract_fusion, f32[128,256]{1,0:T(8,128)S(1)} %fusion.22, f32[128,256]{1,0:T(8,128)S(1)} %fusion.17), kind=kOutput, calls=%fused_computation.30 | convolution fusion | flops 4026597376 | bytes 10747904 | tf_op jit(solution)/shard_map/dot_general | solution.py:42
  358.4 9.3 %pad_maximum_fusion = f32[5120,512]{0,1:T(8,128)} fusion(f32[5120,256]{0,1:T(8,128)} %fusion.10, f32[5120,256]{0,1:T(8,128)} %bitcast.92), kind=kLoop, calls=%fused_computation.8 | loop fusion | flops 2621440 | bytes 20971520 | tf_op jit(solution)/shard_map/concatenate | solution.py:45
  367.7 11.4 %copy.47 = f32[5120,512]{1,0:T(8,128)} copy(f32[5120,512]{0,1:T(8,128)} %pad_maximum_fusion) | data formatting | bytes 20971520 | tf_op jit(solution)/shard_map/concatenate | solution.py:45
  379.1 6.2 %gather_fusion = f32[512,512]{1,0:T(8,128)S(1)} fusion(f32[5120,512]{1,0:T(8,128)} %copy.47, s32[1024]{0:T(1024)S(1)} %pad_clamp_fusion), kind=kCustom, calls=%fused_computation | custom fusion | bytes 2099200 | tf_op jit(solution)/shard_map/jit(_take)/gather | solution.py:121
  386.6 2.0 fusion.7
  388.6 60.0 %all-reduce.6.cloned.1.call-done = f32[512,512]{1,0:T(8,128)} async-done(((f32[512,512]{1,0:T(8,128)}), f32[512,512]{1,0:T(8,128)}) %all-reduce.6.cloned.1.call-update) | async-done | bytes 1048592 | tf_op jit(solution)/shard_map/psum | solution.py:122
  448.6 39.6 %add_subtract_fusion = f32[5120,512]{1,0:T(8,128)} fusion(f32[5120,512]{1,0:T(8,128)} %reshape.199, f32[5120,512]{1,0:T(8,128)} %param.10, f32[5120,512]{1,0:T(8,128)} %reshape.195, f32[512,512]{1,0:T(8,128)} %all-reduce.6.cloned.1.call-done, f32[5120]{0:T(1024)S(1)} %fusion.31, f32[5120,256]{0,1:T(8,128)} %fusion.10, f32[5120,256]{0,1:T(8,128)} %bitcast.94), kind=kOutput, calls=%fused_computation.12 | convolution fusion | flops 16119234560 | bytes 53497856 | tf_op jit(solution)/shard_map/dot_general | solution.py:123
  (90 shorter events, 21.5 us)
Async XLA Ops:
  7.2 10.2 %copy-start.3 = (bf16[512,1024]{1,0:T(8,128)(2,1)S(1)}, bf16[512,1024]{1,0:T(8,128)(2,1)}, u32[]{:S(2)}) copy-start(bf16[512,1024]{1,0:T(8,128)(2,1)} %param.12) | copy-start | bytes 3145732
  7.2 37.2 %copy-start.5 = (s32[32]{0:T(128)S(1)}, s32[32]{0:T(128)}, u32[]{:S(2)}) copy-start(s32[32]{0:T(128)} %param.13) | copy-start | bytes 388
  7.2 37.2 %copy-start.4 = (s32[32]{0:T(128)S(1)}, s32[32]{0:T(128)}, u32[]{:S(2)}) copy-start(s32[32]{0:T(128)} %param.14) | copy-start | bytes 388
  7.2 136.4 %all-gather.2.cloned.1.call-start = ((), (), s32[]{:S(2)}) async-start(), calls=%async_computation.4 | async-start | bytes 11141120 | tf_op jit(solution)/shard_map/all_gather | solution.py:106
  10.2 27.6 %all-to-all-start = ((bf16[512,16,64]{0,2,1:T(8,128)(2,1)}), bf16[512,16,64]{0,2,1:T(8,128)(2,1)S(1)}, u32[]{:S(2)}, u32[]{:S(2)}) async-start(bf16[512,16,64]{0,2,1:T(8,128)(2,1)} %bitcast.11), calls=%async_computation | async-start | bytes 2097152 | tf_op jit(solution)/shard_map/all_to_all | solution.py:75
  37.8 7.0 %copy-start.1 = (bf16[512,16,64]{0,2,1:T(8,128)(2,1)}, bf16[512,16,64]{0,2,1:T(8,128)(2,1)S(1)}, u32[]{:S(2)}) copy-start(bf16[512,16,64]{0,2,1:T(8,128)(2,1)S(1)} %all-to-all-done) | copy-start | bytes 3145732
  37.8 23.7 %all-to-all-start.2 = ((bf16[512,16,64]{0,2,1:T(8,128)(2,1)}), bf16[512,16,64]{0,2,1:T(8,128)(2,1)S(1)}, u32[]{:S(2)}, u32[]{:S(2)}) async-start(bf16[512,16,64]{0,2,1:T(8,128)(2,1)} %bitcast.15), calls=%async_computation.2 | async-start | bytes 2097152 | tf_op jit(solution)/shard_map/all_to_all | solution.py:76
  61.5 33.7 %all-to-all-start.1 = ((bf16[8,2048,64]{1,2,0:T(8,128)(2,1)}), bf16[8,2048,64]{1,2,0:T(8,128)(2,1)S(1)}, u32[]{:S(2)}, u32[]{:S(2)}) async-start(bf16[8,2048,64]{1,2,0:T(8,128)(2,1)} %copy.41), calls=%async_computation.1 | async-start | bytes 4194304 | tf_op jit(solution)/shard_map/all_to_all | solution.py:90
  95.2 35.5 %all-to-all-start.3 = ((bf16[8,2048,64]{1,2,0:T(8,128)(2,1)}), bf16[8,2048,64]{1,2,0:T(8,128)(2,1)}, u32[]{:S(2)}, u32[]{:S(2)}) async-start(bf16[8,2048,64]{1,2,0:T(8,128)(2,1)} %copy.45), calls=%async_computation.3 | async-start | bytes 4194304 | tf_op jit(solution)/shard_map/all_to_all | solution.py:91
  99.6 111.3 %all-reduce.4.cloned.1.call-start = ((), (), s32[]{:S(2)}) async-start(), calls=%async_computation.5 | async-start | bytes 2097152 | tf_op jit(solution)/shard_map/psum | solution.py:12
  146.0 302.6 %all-reduce.6.cloned.1.call-start = ((), (), s32[]{:S(2)}) async-start(), calls=%async_computation.6 | async-start | bytes 2097152 | tf_op jit(solution)/shard_map/psum | solution.py:122
  210.9 62.7 %copy-start.2 = (f32[512,512]{0,1:T(8,128)S(1)}, f32[512,512]{0,1:T(8,128)}, u32[]{:S(2)}) copy-start(f32[512,512]{0,1:T(8,128)} %all-reduce.4.cloned.1.call-done) | copy-start | bytes 3145732
  342.9 9.0 %copy-start = (f32[256,5120]{1,0:T(8,128)}, f32[256,5120]{1,0:T(8,128)S(1)}, u32[]{:S(2)}) copy-start(f32[256,5120]{1,0:T(8,128)S(1)} %fusion.4) | copy-start | bytes 15728644
Sparse Core Ops, SparseCore 0:
  10.2 89.2 all-gather.1
  146.1 64.7 all-reduce.3
  386.7 61.7 all-reduce.5
where the time goes:
time: 502 us; the launch traced here: 495 us
  waiting for transfers between devices  135 us (27%)
  other arithmetic  126 us (25%)
  local copies, waits for them, and re-layouts  107 us (21%)
  matrix products  85.3 us (17%)
  starting transfers between devices  24.9 us (5%)
  between operations  17.2 us (3%)
    another operation x13, other arithmetic, inverse_factor(): lower = jnp.linalg.cholesky(block)  68.6 us
    psum x1, waiting for transfers between devices, per_device(): slab_rows = lax.psum(picked, 'row')  60 us
    psum x1, waiting for transfers between devices, from_root(): return lax.psum(kept, axis)  45.9 us
    another operation x5, other arithmetic, inverse_factor(): return jax.scipy.linalg.solve_triangular(lower, identity, lower=True)  39.8 us
    dot_general x1, matrix products, per_device(): jnp.dot(masked, slab_rows.T, precision=lax.Precision.HIGHEST, preferred_e...  39.6 us
    reshape x2, local copies, waits for them, and re-layouts, place(): return added.reshape(rows_dev, slab_width)  21.5 us
    all_to_all x1, waiting for transfers between devices, per_device(): lax.all_to_all(split_columns(child_one), 'col', split_axis=1, concat_axis...  19.1 us
    all_to_all x3, local copies, waits for them, and re-layouts, per_device(): lax.all_to_all(send_rows(got_two, map_two), 'row', split_axis=0, concat_a...  16.9 us
  transfers between devices with their start and end apart: 7, of which 4 were waited for; matrix products, arithmetic and copies ran while one was open for 18% of the time, Pallas kernels for 0%

commit v1 on v0

--- a/solution.py
+++ b/solution.py
@@ -72,7 +72,15 @@
         return child.reshape(child_local, col_count, piece)
 
     got_one, got_two = (
-        lax.all_to_all(split_columns(child_one), "col", split_axis=1, concat_axis=0, tiled=True),
+        jnp.concatenate(
+            lax.all_to_all(
+                jnp.stack(jnp.split(split_columns(child_one), lax.axis_size("col"), axis=1)),
+                "col",
+                0,
+                0,
+            ),
+            axis=0,
+        ),
         lax.all_to_all(split_columns(child_two), "col", split_axis=1, concat_axis=0, tiled=True),
     )
 

time: 502 us -> 518 us (1.032)
  local copies, waits for them, and re-layouts: 107 us -> 117 us
  waiting for transfers between devices: 135 us -> 145 us
    unnamed x16 -> x31, local copies, waits for them, and re-layouts: 13.7 us -> 22.5 us
    all_to_all x1, waiting for transfers between devices: 0.01 us -> 7.01 us  [per_device(): lax.all_to_all(split_columns(child_two), 'col', split_axis=1, concat_axis...]
  transfers between devices with their start and end apart: 7 -> 7, of which waited for: 4 -> 5; matrix products, arithmetic and copies ran while one was open for 18% -> 20% of each run, Pallas kernels for 0% -> 0%
where the time goes in v1:
time: 518 us; the launch traced here: 510 us
  waiting for transfers between devices  145 us (28%)
  other arithmetic  126 us (24%)
  local copies, waits for them, and re-layouts  117 us (23%)
  matrix products  85.3 us (16%)
  starting transfers between devices  20.4 us (4%)
  between operations  17.2 us (3%)
    another operation x13, other arithmetic, inverse_factor(): lower = jnp.linalg.cholesky(block)  68.6 us
    psum x1, waiting for transfers between devices, per_device(): slab_rows = lax.psum(picked, 'row')  60 us
    psum x1, waiting for transfers between devices, from_root(): return lax.psum(kept, axis)  45.3 us
    another operation x5, other arithmetic, inverse_factor(): return jax.scipy.linalg.solve_triangular(lower, identity, lower=True)  39.8 us
    dot_general x1, matrix products, per_device(): jnp.dot(masked, slab_rows.T, precision=lax.Precision.HIGHEST, preferred_e...  39.6 us
    all_to_all x1, waiting for transfers between devices, per_device(): lax.all_to_all(jnp.stack(jnp.split(split_columns(child_one), lax.axis_siz...  22.9 us
    unnamed x31, local copies, waits for them, and re-layouts  22.5 us
    reshape x2, local copies, waits for them, and re-layouts, place(): return added.reshape(rows_dev, slab_width)  21.6 us
  transfers between devices with their start and end apart: 7, of which 5 were waited for; matrix products, arithmetic and copies ran while one was open for 20% of the time, Pallas kernels for 0%

profile of v1, /device:TPU:0, one launch (start us, length us, event | category | flops | bytes accessed | tf_op | source)
XLA Modules:
  0.0 510.3 jit_solution(7957695563744607867)
XLA Ops:
  19.6 7.1 %all-to-all-start = ((bf16[16,512,1,64]{1,3,2,0:T(8,128)(2,1)}), bf16[16,512,1,64]{1,3,2,0:T(8,128)(2,1)S(1)}, u32[]{:S(2)}, u32[]{:S(2)}) async-start(bf16[16,512,1,64]{1,3,2,0:T(8,128)(2,1)} %fusion.21), calls=%async_computation | async-start | bytes 2097152 | tf_op jit(solution)/shard_map/all_to_all | solution.py:76
  28.1 22.9 %all-to-all-done = bf16[16,512,1,64]{1,3,2,0:T(8,128)(2,1)S(1)} async-done(((bf16[16,512,1,64]{1,3,2,0:T(8,128)(2,1)}), bf16[16,512,1,64]{1,3,2,0:T(8,128)(2,1)S(1)}, u32[]{:S(2)}, u32[]{:S(2)}) %all-to-all-start) | async-done | bytes 1048608 | tf_op jit(solution)/shard_map/all_to_all | solution.py:76
  51.0 3.7 all-to-all-start.2
  55.0 2.0 copy.55
  57.1 2.5 reshape_reshape.3
  59.6 1.9 convolution_convert_fusion.1
  61.5 5.5 %all_to_all.39 = bf16[8,2048,64]{2,1,0:T(8,128)(2,1)} reshape(bf16[64,16384]{1,0:T(8,128)(2,1)S(1)} %convolution_convert_fusion.1) | data formatting | bytes 4194304 | tf_op jit(solution)/shard_map/all_to_all | solution.py:98
  67.0 4.8 copy.56
  71.8 7.0 %all-to-all-done.2 = bf16[512,16,64]{0,2,1:T(8,128)(2,1)S(1)} async-done(((bf16[512,16,64]{0,2,1:T(8,128)(2,1)}), bf16[512,16,64]{0,2,1:T(8,128)(2,1)S(1)}, u32[]{:S(2)}, u32[]{:S(2)}) %all-to-all-start.2) | async-done | bytes 1048608 | tf_op jit(solution)/shard_map/all_to_all | solution.py:84
  78.8 5.0 all-to-all-start.1
  84.2 1.8 copy.59
  86.0 2.8 reshape.192
  88.8 2.0 convolution_convert_fusion
  90.9 6.5 %all_to_all.45 = bf16[8,2048,64]{2,1,0:T(8,128)(2,1)} reshape(bf16[64,16384]{1,0:T(8,128)(2,1)} %convolution_convert_fusion) | data formatting | bytes 4194304 | tf_op jit(solution)/shard_map/all_to_all | solution.py:99
  97.4 4.8 copy.60
  102.1 8.9 %all-to-all-done.1 = bf16[8,2048,64]{1,2,0:T(8,128)(2,1)S(1)} async-done(((bf16[8,2048,64]{1,2,0:T(8,128)(2,1)}), bf16[8,2048,64]{1,2,0:T(8,128)(2,1)S(1)}, u32[]{:S(2)}, u32[]{:S(2)}) %all-to-all-start.1) | async-done | bytes 2097184 | tf_op jit(solution)/shard_map/all_to_all | solution.py:98
  111.0 4.3 all-to-all-start.3
  116.6 4.2 copy.57
  120.8 5.0 reshape.227
  125.8 2.2 reshape.189
  128.0 7.9 %fusion.54 = f32[20,131072]{1,0:T(8,128)} fusion(bf16[8,131072]{1,0:T(8,128)(2,1)} %reshape.189, s32[20,8]{1,0:T(8,128)S(1)} %convert_reduce_fusion.1), kind=kOutput, calls=%fused_computation.118 | convolution fusion | flops 41943200 | bytes 12583552 | tf_op jit(solution)/shard_map/dot_general | solution.py:108
  136.0 10.5 %reshape.190 = f32[5120,512]{1,0:T(8,128)} reshape(f32[20,131072]{1,0:T(8,128)} %fusion.54) | data formatting | bytes 20971520 | tf_op jit(solution)/shard_map/reshape | solution.py:111
  146.5 5.6 %copy.61 = bf16[2048,8,64]{2,1,0:T(8,128)(2,1)} copy(bf16[2048,8,64]{0,2,1:T(8,128)(2,1)} %bitcast.32) | data formatting | bytes 4194304 | tf_op jit(solution)/shard_map/all_to_all | solution.py:99
  152.1 5.0 reshape.225
  157.2 2.2 reshape.193
  159.4 2.3 slice_select_fusion
  161.8 7.9 %fusion.52 = f32[20,131072]{1,0:T(8,128)} fusion(bf16[8,131072]{1,0:T(8,128)(2,1)} %reshape.193, s32[20,8]{1,0:T(8,128)S(1)} %convert_reduce_fusion), kind=kOutput, calls=%fused_computation.116 | convolution fusion | flops 41943200 | bytes 12583552 | tf_op jit(solution)/shard_map/dot_general | solution.py:108
  169.7 11.1 %reshape.194 = f32[5120,512]{1,0:T(8,128)} reshape(f32[20,131072]{1,0:T(8,128)} %fusion.52) | data formatting | bytes 20971520 | tf_op jit(solution)/shard_map/reshape | solution.py:111
  180.8 45.3 %all-reduce.4.cloned.1.call-done = f32[512,512]{0,1:T(8,128)} async-done(((f32[512,512]{0,1:T(8,128)}), f32[512,512]{0,1:T(8,128)}) %all-reduce.4.cloned.1.call-update) | async-done | bytes 1048592 | tf_op jit(solution)/shard_map/psum | solution.py:12
  228.2 11.7 %cholesky.130 = f32[128,128]{1,0:T(8,128)S(1)} custom-call(f32[128,128]{1,0:T(8,128)S(1)} %cholesky.194), custom_call_target="Cholesky" | custom-call | tf_op jit(solution)/shard_map/jit(cholesky)/cholesky | solution.py:16
  240.0 9.8 %custom-call.13 = f32[1,128,128]{1,2,0:T(8,128)S(1)} custom-call(f32[1,128,128]{2,1,0:T(8,128)S(1)} %get-tuple-element.51), custom_call_target="InvertDiagBlocksLowerTriangular" | custom-call | tf_op jit(solution)/shard_map/jit(cholesky)/cholesky | solution.py:16
  250.3 11.7 %cholesky.147 = f32[128,128]{1,0:T(8,128)S(1)} custom-call(f32[128,128]{1,0:T(8,128)S(1)} %convolution_subtract_fusion.5), custom_call_target="Cholesky" | custom-call | tf_op jit(solution)/shard_map/jit(cholesky)/cholesky | solution.py:16
  264.1 3.9 while.4
  267.9 19.8 %custom-call.14 = f32[2,128,128]{1,2,0:T(8,128)S(1)} custom-call(f32[2,128,128]{2,1,0:T(8,128)S(1)} %get-tuple-element.18), custom_call_target="InvertDiagBlocksLowerTriangular" | custom-call | tf_op jit(solution)/shard_map/jit(_solve_triangular)/triangular_solve | solution.py:18
  289.9 11.7 %cholesky.164 = f32[128,128]{1,0:T(8,128)S(1)} custom-call(f32[128,128]{1,0:T(8,128)S(1)} %cholesky.197), custom_call_target="Cholesky" | custom-call | tf_op jit(solution)/shard_map/jit(cholesky)/cholesky | solution.py:16
  301.7 9.8 %custom-call.15 = f32[1,128,128]{1,2,0:T(8,128)S(1)} custom-call(f32[1,128,128]{2,1,0:T(8,128)S(1)} %get-tuple-element.47), custom_call_target="InvertDiagBlocksLowerTriangular" | custom-call | tf_op jit(solution)/shard_map/jit(cholesky)/cholesky | solution.py:16
  312.0 11.7 %cholesky.181 = f32[128,128]{1,0:T(8,128)S(1)} custom-call(f32[128,128]{1,0:T(8,128)S(1)} %convolution_subtract_fusion.4), custom_call_target="Cholesky" | custom-call | tf_op jit(solution)/shard_map/jit(cholesky)/cholesky | solution.py:16
  326.5 4.1 while.5
  330.5 19.9 %custom-call.16 = f32[2,128,128]{1,2,0:T(8,128)S(1)} custom-call(f32[2,128,128]{2,1,0:T(8,128)S(1)} %get-tuple-element.19), custom_call_target="InvertDiagBlocksLowerTriangular" | custom-call | tf_op jit(solution)/shard_map/jit(_solve_triangular)/triangular_solve | solution.py:18
  351.3 6.7 %fusion.4 = f32[256,5120]{1,0:T(8,128)S(1)} fusion(f32[5120,512]{0,1:T(8,128)} %all-gather.2.cloned.1.call-done, f32[128,256]{1,0:T(8,128)S(1)} %fusion.42, f32[128,256]{1,0:T(8,128)S(1)} %fusion.19), kind=kOutput, calls=%fused_computation.14 | convolution fusion | flops 4026597376 | bytes 10747904 | tf_op jit(solution)/shard_map/dot_general | solution.py:36
  358.0 9.0 %convolution_subtract_fusion = f32[5120,256]{0,1:T(8,128)S(1)} fusion(f32[256,5120]{1,0:T(8,128)S(1)} %fusion.4, f32[256,256]{1,0:T(8,128)S(1)} %fusion.8, f32[5120,512]{0,1:T(8,128)} %all-gather.2.cloned.1.call-done), kind=kOutput, calls=%fused_computation.13 | convolution fusion | flops 4027842560 | bytes 15990784 | tf_op jit(solution)/shard_map/dot_general | solution.py:39
  367.0 6.5 %fusion.10 = f32[5120,256]{0,1:T(8,128)} fusion(f32[5120,256]{0,1:T(8,128)S(1)} %convolution_subtract_fusion, f32[128,256]{1,0:T(8,128)S(1)} %fusion.38, f32[128,256]{1,0:T(8,128)S(1)} %fusion.17), kind=kOutput, calls=%fused_computation.30 | convolution fusion | flops 4026597376 | bytes 10747904 | tf_op jit(solution)/shard_map/dot_general | solution.py:42
  373.6 9.3 %pad_maximum_fusion = f32[5120,512]{0,1:T(8,128)} fusion(f32[5120,256]{0,1:T(8,128)} %fusion.10, f32[5120,256]{0,1:T(8,128)} %bitcast.153), kind=kLoop, calls=%fused_computation.8 | loop fusion | flops 2621440 | bytes 20971520 | tf_op jit(solution)/shard_map/concatenate | solution.py:45
  382.9 11.4 %copy.62 = f32[5120,512]{1,0:T(8,128)} copy(f32[5120,512]{0,1:T(8,128)} %pad_maximum_fusion) | data formatting | bytes 20971520 | tf_op jit(solution)/shard_map/concatenate | solution.py:45
  394.3 6.2 %gather_fusion = f32[512,512]{1,0:T(8,128)S(1)} fusion(f32[5120,512]{1,0:T(8,128)} %copy.62, s32[1024]{0:T(1024)S(1)} %pad_clamp_fusion), kind=kCustom, calls=%fused_computation | custom fusion | bytes 2099200 | tf_op jit(solution)/shard_map/jit(_take)/gather | solution.py:129
  401.8 2.0 fusion.7
  403.8 60.0 %all-reduce.6.cloned.1.call-done = f32[512,512]{1,0:T(8,128)} async-done(((f32[512,512]{1,0:T(8,128)}), f32[512,512]{1,0:T(8,128)}) %all-reduce.6.cloned.1.call-update) | async-done | bytes 1048592 | tf_op jit(solution)/shard_map/psum | solution.py:130
  463.8 39.6 %add_subtract_fusion = f32[5120,512]{1,0:T(8,128)} fusion(f32[5120,512]{1,0:T(8,128)} %reshape.194, f32[5120,512]{1,0:T(8,128)} %param.10, f32[5120,512]{1,0:T(8,128)} %reshape.190, f32[512,512]{1,0:T(8,128)} %all-reduce.6.cloned.1.call-done, f32[5120]{0:T(1024)S(1)} %fusion.47, f32[5120,256]{0,1:T(8,128)} %fusion.10, f32[5120,256]{0,1:T(8,128)} %bitcast.155), kind=kOutput, calls=%fused_computation.12 | convolution fusion | flops 16119234560 | bytes 53497856 | tf_op jit(solution)/shard_map/dot_general | solution.py:131
  (106 shorter events, 33.1 us)
Async XLA Ops:
  7.2 19.6 %copy-start.3 = (bf16[512,1024]{1,0:T(8,128)(2,1)S(1)}, bf16[512,1024]{1,0:T(8,128)(2,1)}, u32[]{:S(2)}) copy-start(bf16[512,1024]{1,0:T(8,128)(2,1)} %param.12) | copy-start | bytes 3145732
  7.2 152.2 %all-gather.2.cloned.1.call-start = ((), (), s32[]{:S(2)}) async-start(), calls=%async_computation.4 | async-start | bytes 11141120 | tf_op jit(solution)/shard_map/all_gather | solution.py:114
  7.9 46.8 %copy-start.4 = (s32[32]{0:T(128)S(1)}, s32[32]{0:T(128)}, u32[]{:S(2)}) copy-start(s32[32]{0:T(128)} %param.14) | copy-start | bytes 388
  7.9 46.8 %copy-start.5 = (s32[32]{0:T(128)S(1)}, s32[32]{0:T(128)}, u32[]{:S(2)}) copy-start(s32[32]{0:T(128)} %param.13) | copy-start | bytes 388
  19.6 31.4 %all-to-all-start = ((bf16[16,512,1,64]{1,3,2,0:T(8,128)(2,1)}), bf16[16,512,1,64]{1,3,2,0:T(8,128)(2,1)S(1)}, u32[]{:S(2)}, u32[]{:S(2)}) async-start(bf16[16,512,1,64]{1,3,2,0:T(8,128)(2,1)} %fusion.21), calls=%async_computation | async-start | bytes 2097152 | tf_op jit(solution)/shard_map/all_to_all | solution.py:76
  51.0 4.0 copy-start.1
  51.0 27.8 %all-to-all-start.2 = ((bf16[512,16,64]{0,2,1:T(8,128)(2,1)}), bf16[512,16,64]{0,2,1:T(8,128)(2,1)S(1)}, u32[]{:S(2)}, u32[]{:S(2)}) async-start(bf16[512,16,64]{0,2,1:T(8,128)(2,1)} %bitcast.29), calls=%async_computation.2 | async-start | bytes 2097152 | tf_op jit(solution)/shard_map/all_to_all | solution.py:84
  78.8 32.2 %all-to-all-start.1 = ((bf16[8,2048,64]{1,2,0:T(8,128)(2,1)}), bf16[8,2048,64]{1,2,0:T(8,128)(2,1)S(1)}, u32[]{:S(2)}, u32[]{:S(2)}) async-start(bf16[8,2048,64]{1,2,0:T(8,128)(2,1)} %copy.56), calls=%async_computation.1 | async-start | bytes 4194304 | tf_op jit(solution)/shard_map/all_to_all | solution.py:98
  111.0 35.5 %all-to-all-start.3 = ((bf16[8,2048,64]{1,2,0:T(8,128)(2,1)}), bf16[8,2048,64]{1,2,0:T(8,128)(2,1)}, u32[]{:S(2)}, u32[]{:S(2)}) async-start(bf16[8,2048,64]{1,2,0:T(8,128)(2,1)} %copy.60), calls=%async_computation.3 | async-start | bytes 4194304 | tf_op jit(solution)/shard_map/all_to_all | solution.py:99
  115.4 110.7 %all-reduce.4.cloned.1.call-start = ((), (), s32[]{:S(2)}) async-start(), calls=%async_computation.5 | async-start | bytes 2097152 | tf_op jit(solution)/shard_map/psum | solution.py:12
  161.7 302.0 %all-reduce.6.cloned.1.call-start = ((), (), s32[]{:S(2)}) async-start(), calls=%async_computation.6 | async-start | bytes 2097152 | tf_op jit(solution)/shard_map/psum | solution.py:130
  226.0 62.7 %copy-start.2 = (f32[512,512]{0,1:T(8,128)S(1)}, f32[512,512]{0,1:T(8,128)}, u32[]{:S(2)}) copy-start(f32[512,512]{0,1:T(8,128)} %all-reduce.4.cloned.1.call-done) | copy-start | bytes 3145732
  358.0 9.0 %copy-start = (f32[256,5120]{1,0:T(8,128)}, f32[256,5120]{1,0:T(8,128)S(1)}, u32[]{:S(2)}) copy-start(f32[256,5120]{1,0:T(8,128)S(1)} %fusion.4) | copy-start | bytes 15728644
Sparse Core Ops, SparseCore 0:
  10.2 101.6 all-gather.1
  161.8 64.1 all-reduce.3
  401.9 61.8 all-reduce.5
